TPU v7x, 1024 devices: a whole 4x4x32 slice. The times are simulated.
1024 devices in a mesh: dp: 16 (over z_hi, y), expert: 16 (over z_lo, core), tp: 4 (over x).
Axes of the slice: x: 4, y: 4, z: 32 (z_hi: 4, z_lo: 8; z = z_hi * 8 + z_lo), core: 2. Of those that a mesh axis runs over, the one named last changes fastest.
Arguments:
- tokens: bfloat16 [2048, 3584], P(('dp', 'expert'), 'tp'), may hold values from -6 to 6
- out_grad: bfloat16 [2048, 3584], P(('dp', 'expert'), 'tp'), may hold values from -6 to 6
- expert_ids: int32 [2048, 2], P(('dp', 'expert')), may hold values from 0 to 15, all different within a row; in each aligned block of 8 rows (0 to 7, 8 to 15, ...) at most 2 rows name the same one
- gate_probs: float32 [2048, 2], P(('dp', 'expert')), may hold values from 0.1 to 1
- w_gate: bfloat16 [16, 3584, 4864], P('expert', 'tp', 'dp'), may hold values from -0.09375 to 0.09375
- w_up: bfloat16 [16, 3584, 4864], P('expert', 'tp', 'dp'), may hold values from -0.09375 to 0.09375
- w_down: bfloat16 [16, 4864, 3584], P('expert', 'dp', 'tp'), may hold values from -0.078125 to 0.078125
Outputs:
- mixed: bfloat16 [2048, 3584], P(('dp', 'expert'), 'tp')
- grad_tokens: bfloat16 [2048, 3584], P(('dp', 'expert'), 'tp')
- grad_gate: bfloat16 [16, 3584, 4864], P('expert', 'tp', 'dp')
- grad_up: bfloat16 [16, 3584, 4864], P('expert', 'tp', 'dp')
- grad_down: bfloat16 [16, 4864, 3584], P('expert', 'dp', 'tp')
Inputs may be any that keep to these rules, and one draw needn't show every extreme that they name: `expert_ids`: the two ids of a token differ. In each aligned block of 8 tokens (the tokens of one device) no expert is named by more than 2 tokens, a bound that some block reaches.
All inputs are finite; a program needn't handle non-finite values.
Results may differ from a plain program's by a relative error of at most 0.0065.
Values may be sent and summed in bfloat16 or wider, within the bound.
A program may use at most 32 MiB of HBM per device.

v0:
```python
import jax
import jax.numpy as jnp
from jax import lax
from jax.sharding import PartitionSpec as P


def slot_within(identity, experts):
    matches = (identity[:, :, None] == jnp.arange(experts, dtype=jnp.int32)[None, None, :]).astype(
        jnp.int32
    )
    before = jnp.cumsum(matches, axis=1) - matches
    return jnp.sum(before * matches, axis=2)


def contract_rows(left, right):
    return lax.dot_general(
        left, right, (((0,), (0,)), ((), ())), preferred_element_type=jnp.float32
    )


def contract_cols(left, right):
    return lax.dot_general(
        left, right, (((1,), (1,)), ((), ())), preferred_element_type=jnp.float32
    )


def shards(tokens, out_grad, expert_ids, gate_probs, w_gate, w_up, w_down):
    tok_rows = tokens.shape[0]
    quarter = tokens.shape[1]
    experts = lax.axis_size("expert") * w_gate.shape[0]
    capacity = max(2, 4 * tok_rows // experts)
    slot_total = experts * capacity
    within = slot_within(expert_ids.reshape(1, tok_rows * 2), experts).reshape(tok_rows, 2)
    target = expert_ids * capacity + within
    columns = jnp.arange(slot_total, dtype=jnp.int32)
    matched = (target[:, :, None] == columns[None, None, :]).astype(jnp.float32)
    placing = jnp.sum(matched, axis=1)
    weighing = jnp.sum(matched * gate_probs[:, :, None], axis=1)
    x_send = contract_rows(placing.astype(jnp.bfloat16), tokens).astype(jnp.bfloat16)
    dy_send = lax.dot_general(
        weighing,
        out_grad.astype(jnp.float32),
        (((0,), (0,)), ((), ())),
        precision=lax.Precision.HIGHEST,
        preferred_element_type=jnp.float32,
    ).astype(jnp.bfloat16)
    shaped = (experts, capacity, quarter)
    x_recv, dy_recv = (
        lax.all_to_all(x_send.reshape(shaped), "expert", split_axis=0, concat_axis=0, tiled=True),
        lax.all_to_all(dy_send.reshape(shaped), "expert", split_axis=0, concat_axis=0, tiled=True),
    )
    x_local = x_recv.reshape(slot_total, quarter)
    dy_local = dy_recv.reshape(slot_total, quarter)
    x_rows, dy_rows = (
        lax.all_gather(x_local, "dp", axis=0, tiled=True),
        lax.all_gather(dy_local, "dp", axis=0, tiled=True),
    )
    gate_loc = w_gate[0]
    up_loc = w_up[0]
    down_loc = w_down[0]
    gate_part = jnp.dot(x_rows, gate_loc, preferred_element_type=jnp.float32)
    up_part = jnp.dot(x_rows, up_loc, preferred_element_type=jnp.float32)
    gate_sum, up_sum = lax.psum((gate_part, up_part), "tp")
    sigmoid_gate = jax.nn.sigmoid(gate_sum)
    swish_gate = gate_sum * sigmoid_gate
    hidden = (swish_gate * up_sum).astype(jnp.bfloat16)
    out_rows = lax.psum_scatter(
        jnp.dot(hidden, down_loc, preferred_element_type=jnp.float32),
        "dp",
        scatter_dimension=0,
        tiled=True,
    ).astype(jnp.bfloat16)
    back_part = contract_cols(dy_rows, down_loc)
    back_hidden = lax.psum(back_part, "tp")
    slope = sigmoid_gate * (1.0 + gate_sum * (1.0 - sigmoid_gate))
    grad_gate_rows = (back_hidden * up_sum * slope).astype(jnp.bfloat16)
    grad_up_rows = (back_hidden * swish_gate).astype(jnp.bfloat16)
    in_rows = lax.psum_scatter(
        contract_cols(grad_gate_rows, gate_loc) + contract_cols(grad_up_rows, up_loc),
        "dp",
        scatter_dimension=0,
        tiled=True,
    ).astype(jnp.bfloat16)
    grad_gate = contract_rows(x_rows, grad_gate_rows).astype(jnp.bfloat16)[None]
    grad_up = contract_rows(x_rows, grad_up_rows).astype(jnp.bfloat16)[None]
    grad_down = contract_rows(hidden, dy_rows).astype(jnp.bfloat16)[None]
    back_out, back_in = (
        lax.all_to_all(out_rows.reshape(shaped), "expert", split_axis=0, concat_axis=0, tiled=True),
        lax.all_to_all(in_rows.reshape(shaped), "expert", split_axis=0, concat_axis=0, tiled=True),
    )
    mixed = jnp.dot(
        weighing,
        back_out.reshape(slot_total, quarter).astype(jnp.float32),
        precision=lax.Precision.HIGHEST,
        preferred_element_type=jnp.float32,
    )
    grad_tokens = jnp.dot(
        placing,
        back_in.reshape(slot_total, quarter).astype(jnp.float32),
        precision=lax.Precision.HIGHEST,
        preferred_element_type=jnp.float32,
    )
    return (
        mixed.astype(jnp.bfloat16),
        grad_tokens.astype(jnp.bfloat16),
        grad_gate,
        grad_up,
        grad_down,
    )


def solution(mesh):
    placed = (
        P(("dp", "expert"), "tp"),
        P(("dp", "expert"), "tp"),
        P(("dp", "expert"), None),
        P(("dp", "expert"), None),
        P("expert", "tp", "dp"),
        P("expert", "tp", "dp"),
        P("expert", "dp", "tp"),
    )
    return jax.shard_map(
        shards,
        mesh=mesh,
        in_specs=placed,
        out_specs=(
            P(("dp", "expert"), "tp"),
            P(("dp", "expert"), "tp"),
            P("expert", "tp", "dp"),
            P("expert", "tp", "dp"),
            P("expert", "dp", "tp"),
        ),
        check_vma=False,
    )
```

profile of v0, /device:TPU:1, one launch (start us, length us, event | category | flops | bytes accessed | tf_op | source)
XLA Modules:
  0.0 801.0 jit_solution(15081712253110492267)
XLA Ops:
  7.2 0.8 copy.18
  8.6 0.8 convert_reduce_fusion
  9.4 0.9 convolution_convert_fusion.4
  10.3 0.7 reshape.133
  10.9 17.4 %all-to-all-start = ((bf16[16,2,896]{2,1,0:T(2,128)(2,1)}), bf16[16,2,896]{2,1,0:T(2,128)(2,1)S(1)}, u32[]{:S(2)}, u32[]{:S(2)}) async-start(bf16[16,2,896]{2,1,0:T(2,128)(2,1)} %reshape.133), calls=%async_computation | async-start | bytes 114688 | tf_op jit(solution)/shard_map/all_to_all | solution.py:49
  28.4 1.0 convolution_convert_fusion.3
  29.3 0.7 reshape.137
  30.0 8.4 %all-to-all-done = bf16[16,2,896]{2,1,0:T(2,128)(2,1)S(1)} async-done(((bf16[16,2,896]{2,1,0:T(2,128)(2,1)}), bf16[16,2,896]{2,1,0:T(2,128)(2,1)S(1)}, u32[]{:S(2)}, u32[]{:S(2)}) %all-to-all-start) | async-done | bytes 57376 | tf_op jit(solution)/shard_map/all_to_all | solution.py:49
  38.4 4.2 all-to-all-start.2
  42.7 116.8 %all_gather.6 = bf16[512,896]{1,0:T(8,128)(2,1)S(1)} all-gather(bf16[32,896]{1,0:T(8,128)(2,1)S(1)} %reshape.134), channel_id=1, replica_groups=mesh['dp'=16,'expert'=16,'tp'=4] {'dp'}, dimensions={0}, use_global_device_ids=true | all-gather | bytes 974848 | tf_op jit(solution)/shard_map/all_gather | solution.py:55
  159.5 1.3 fusion.9
  160.9 1.4 fusion.13
  162.3 94.9 %all_gather.7 = bf16[512,896]{1,0:T(8,128)(2,1)S(1)} all-gather(bf16[32,896]{1,0:T(8,128)(2,1)S(1)} %reshape.138), channel_id=1, replica_groups=mesh['dp'=16,'expert'=16,'tp'=4] {'dp'}, dimensions={0}, use_global_device_ids=true | all-gather | bytes 974848 | tf_op jit(solution)/shard_map/all_gather | solution.py:56
  257.1 1.3 fusion.4
  258.6 96.2 %all-reduce.3.cloned.1.call-done = (f32[512,304]{0,1:T(8,128)}, f32[512,304]{0,1:T(8,128)}, f32[512,304]{0,1:T(8,128)}) async-done(((f32[512,304]{0,1:T(8,128)}, f32[512,304]{0,1:T(8,128)}, f32[512,304]{0,1:T(8,128)}), (f32[512,304]{0,1:T(8,128)}, f32[512,304]{0,1:T(8,128)}, f32[512,304]{0,1:T(8,128)})) %all-reduce.3.cloned.1.call-update) | async-done | bytes 1867792 | tf_op jit(solution)/shard_map/psum | solution.py:63
  354.8 1.9 multiply_convert_fusion
  356.7 0.7 fusion.11
  357.7 1.9 convolution_add_fusion
  359.7 3.0 fusion.6
  362.8 205.6 %reduce-scatter.5.cloned.1.call-done = f32[32,896]{1,0:T(8,128)} async-done(((f32[512,896]{1,0:T(8,128)}), f32[32,896]{1,0:T(8,128)}) %reduce-scatter.5.cloned.1.call-update) | async-done | bytes 114704 | tf_op jit(solution)/shard_map/reduce_scatter | solution.py:78
  568.4 0.9 convert_element_type.70
  569.3 0.7 reshape.139
  570.0 9.1 %all-to-all-start.3 = ((bf16[16,2,896]{2,1,0:T(2,128)(2,1)}), bf16[16,2,896]{2,1,0:T(2,128)(2,1)S(1)}, u32[]{:S(2)}, u32[]{:S(2)}) async-start(bf16[16,2,896]{2,1,0:T(2,128)(2,1)} %reshape.139), calls=%async_computation.5 | async-start | bytes 114688 | tf_op jit(solution)/shard_map/all_to_all | solution.py:89
  579.1 1.3 fusion
  580.4 192.5 %reduce-scatter.3.cloned.1.call-done = f32[32,896]{1,0:T(8,128)} async-done(((f32[512,896]{1,0:T(8,128)}), f32[32,896]{1,0:T(8,128)}) %reduce-scatter.3.cloned.1.call-update) | async-done | bytes 114704 | tf_op jit(solution)/shard_map/reduce_scatter | solution.py:67
  772.9 0.9 convert_element_type.65
  774.5 9.2 %all-to-all-start.1 = ((bf16[16,2,896]{2,1,0:T(2,128)(2,1)}), bf16[16,2,896]{2,1,0:T(2,128)(2,1)S(1)}, u32[]{:S(2)}, u32[]{:S(2)}) async-start(bf16[16,2,896]{2,1,0:T(2,128)(2,1)} %reshape.135), calls=%async_computation.2 | async-start | bytes 114688 | tf_op jit(solution)/shard_map/all_to_all | solution.py:88
  783.7 1.3 fusion.2
  785.0 1.3 fusion.1
  786.3 0.8 convolution_convert_fusion.5
  787.1 6.6 all-to-all-done.1
  793.7 0.7 convolution_convert_fusion.6
  (28 shorter events, 1.8 us)
Async XLA Ops:
  7.2 153.7 %copy-start = (bf16[1,896,304]{1,2,0:T(8,128)(2,1)S(1)}, bf16[1,896,304]{1,2,0:T(8,128)(2,1)}, u32[]{:S(2)}) copy-start(bf16[1,896,304]{1,2,0:T(8,128)(2,1)} %param.11) | copy-start | bytes 1634308
  7.2 152.3 %copy-start.1 = (bf16[1,896,304]{1,2,0:T(8,128)(2,1)S(1)}, bf16[1,896,304]{1,2,0:T(8,128)(2,1)}, u32[]{:S(2)}) copy-start(bf16[1,896,304]{1,2,0:T(8,128)(2,1)} %param.12) | copy-start | bytes 1634308
  10.9 27.5 %all-to-all-start = ((bf16[16,2,896]{2,1,0:T(2,128)(2,1)}), bf16[16,2,896]{2,1,0:T(2,128)(2,1)S(1)}, u32[]{:S(2)}, u32[]{:S(2)}) async-start(bf16[16,2,896]{2,1,0:T(2,128)(2,1)} %reshape.133), calls=%async_computation | async-start | bytes 114688 | tf_op jit(solution)/shard_map/all_to_all | solution.py:49
  38.4 123.8 %all-to-all-start.2 = ((bf16[16,2,896]{2,1,0:T(2,128)(2,1)}), bf16[16,2,896]{2,1,0:T(2,128)(2,1)S(1)}, u32[]{:S(2)}, u32[]{:S(2)}) async-start(bf16[16,2,896]{2,1,0:T(2,128)(2,1)} %reshape.137), calls=%async_computation.3 | async-start | bytes 114688 | tf_op jit(solution)/shard_map/all_to_all | solution.py:50
  42.7 312.1 %all-reduce.3.cloned.1.call-start = ((), (), s32[]{:S(2)}) async-start(), calls=%async_computation.8 | async-start | bytes 3735552 | tf_op jit(solution)/shard_map/psum | solution.py:63
  160.9 96.3 %copy-start.3 = (bf16[1,304,896]{2,1,0:T(8,128)(2,1)S(1)}, bf16[1,304,896]{2,1,0:T(8,128)(2,1)}, u32[]{:S(2)}) copy-start(bf16[1,304,896]{2,1,0:T(8,128)(2,1)} %param.13) | copy-start | bytes 1634308
  258.5 309.9 %reduce-scatter.5.cloned.1.call-start = ((), (), s32[]{:S(2)}) async-start(), calls=%async_computation.7 | async-start | bytes 1949696 | tf_op jit(solution)/shard_map/reduce_scatter | solution.py:78
  356.7 1.1 copy-start.2
  359.7 413.2 %reduce-scatter.3.cloned.1.call-start = ((), (), s32[]{:S(2)}) async-start(), calls=%async_computation.6 | async-start | bytes 1949696 | tf_op jit(solution)/shard_map/reduce_scatter | solution.py:67
  570.0 204.5 %all-to-all-start.3 = ((bf16[16,2,896]{2,1,0:T(2,128)(2,1)}), bf16[16,2,896]{2,1,0:T(2,128)(2,1)S(1)}, u32[]{:S(2)}, u32[]{:S(2)}) async-start(bf16[16,2,896]{2,1,0:T(2,128)(2,1)} %reshape.139), calls=%async_computation.5 | async-start | bytes 114688 | tf_op jit(solution)/shard_map/all_to_all | solution.py:89
  774.5 19.2 %all-to-all-start.1 = ((bf16[16,2,896]{2,1,0:T(2,128)(2,1)}), bf16[16,2,896]{2,1,0:T(2,128)(2,1)S(1)}, u32[]{:S(2)}, u32[]{:S(2)}) async-start(bf16[16,2,896]{2,1,0:T(2,128)(2,1)} %reshape.135), calls=%async_computation.2 | async-start | bytes 114688 | tf_op jit(solution)/shard_map/all_to_all | solution.py:88
Sparse Core Ops, SparseCore 0:
  258.6 96.1 all-reduce.2
  360.1 208.3 reduce-scatter.4
  573.7 199.1 reduce-scatter.2
where the time goes:
time: 802 us; the launch traced here: 801 us
  waiting for transfers between devices  509 us (63%)
  blocking collectives  212 us (26%)
  starting transfers between devices  40.2 us (5%)
  matrix products  17 us (2%)
  between operations  13.8 us (2%)
    reduce_scatter x1, waiting for transfers between devices, shards(): lax.psum_scatter(contract_cols(grad_gate_rows, gate_loc) + contract_cols(...  206 us
    reduce_scatter x1, waiting for transfers between devices, shards(): lax.psum_scatter(jnp.dot(hidden, down_loc, preferred_element_type=jnp.flo...  193 us
    all_gather x1, blocking collectives, shards(): lax.all_gather(x_local, 'dp', axis=0, tiled=True)  117 us
    psum x1, waiting for transfers between devices, shards(): gate_sum, up_sum = lax.psum((gate_part, up_part), 'tp')  96.2 us
    all_gather x1, blocking collectives, shards(): lax.all_gather(dy_local, 'dp', axis=0, tiled=True)  94.9 us
    all_to_all x1, starting transfers between devices, shards(): lax.all_to_all(x_send.reshape(shaped), 'expert', split_axis=0, concat_axi...  17.4 us
  transfers between devices with their start and end apart: 7, of which 5 were waited for; matrix products, arithmetic and copies ran while one was open for 2% of the time, Pallas kernels for 0%

commit v1 on v0

v1 whole, which is shorter than its diff:
```python
import jax
import jax.numpy as jnp
from jax import lax
from jax.experimental import pallas as pl
from jax.experimental.pallas import tpu as pltpu
from jax.sharding import PartitionSpec as P

MESH = pl.DeviceIdType.MESH
BF = jnp.bfloat16
F32 = jnp.float32


def nn(a, b):
    return lax.dot_general(a, b, (((1,), (0,)), ((), ())), preferred_element_type=F32)


def nt(a, b):
    return lax.dot_general(a, b, (((1,), (1,)), ((), ())), preferred_element_type=F32)


def tn(a, b):
    return lax.dot_general(a, b, (((0,), (0,)), ((), ())), preferred_element_type=F32)


def flip(a):
    return a.astype(F32).T.astype(BF)


def kernel(
    tok_ref, og_ref, meta_ref, wg_ref, wu_ref, wd_ref,
    mixed_ref, gtok_ref, gg_ref, gu_ref, gd_ref,
    zed, sx, xd, ps, rp, hb, os_, ro, sb, rb, ts, rs, ta, ra,
    a_s, a_r, s_s, s_r, b_s, b_r, y_s, y_r, p_s, p_r, h_s, h_r,
    o_s, o_r, c_s, c_r, t_s, t_r, f_s, f_r,
):
    dp = lax.axis_index("dp")
    ex = lax.axis_index("expert")
    t = lax.axis_index("tp")
    zh, y, cl, c = dp // 4, dp % 4, ex // 2, ex % 2
    z = zh * 8 + cl
    sc = 1 - c

    def at_z(k):
        zz = (z + k + 32) % 32
        return ((zz // 8) * 4 + y, (zz % 8) * 2 + c, t)

    def at_y(yy):
        return (zh * 4 + yy, ex, t)

    def at_x(tt):
        return (dp, ex, tt)

    sib = (dp, cl * 2 + sc, t)

    def rdma(src, dst, ss, rr, to):
        return pltpu.make_async_remote_copy(
            src, dst, ss, rr, device_id=to, device_id_type=MESH
        )

    peers = [at_z(k) for k in (8, -8, 16, 1, -1, 2, -2, 3, -3, 4, -4)]
    peers += [sib]
    peers += [at_y((y + k) % 4) for k in (1, 2, 3)]
    peers += [at_x((t + k) % 4) for k in (1, 2, 3)]
    bar = pltpu.get_barrier_semaphore()
    for p in peers:
        pl.semaphore_signal(bar, inc=1, device_id=p, device_id_type=MESH)

    zed[zh, c, :, 0:896] = jnp.concatenate([tok_ref[...], og_ref[...]], axis=0)
    zed[zh, c, :, 896:1024] = meta_ref[...]
    pl.semaphore_wait(bar, len(peers))

    pend = []

    def go(copy):
        copy.start()
        pend.append(copy)
        return copy

    ac = {}
    for k in (2, 1, 3):
        me = zed.at[zh, c]
        ac[k] = go(rdma(me, me, a_s.at[k], a_r.at[k], at_z(8 * k)))
    sc_copies = []
    for k in (0, 1, 3, 2):
        src = (zh + 4 - k) % 4
        if k:
            ac[k].wait_recv()
        blk = zed.at[src, c]
        sc_copies.append(go(rdma(blk, blk, s_s.at[k], s_r.at[k], sib)))
    for q in sc_copies:
        q.wait_recv()

    meta = jnp.zeros((16, 128), F32)
    for j in range(4):
        for cc in range(2):
            meta = meta + zed[j, cc, :, 896:1024].astype(F32)
    rid = (lax.broadcasted_iota(jnp.int32, (128, 128), 0) + 1 + 128 * c).astype(F32)
    first = rid == meta[0:1, :]
    second = rid == meta[1:2, :]
    one = jnp.where(first | second, 1.0, 0.0)
    weights = [
        jnp.where(first, meta[2 + i : 3 + i, :], 0.0)
        + jnp.where(second, meta[5 + i : 6 + i, :], 0.0)
        for i in range(3)
    ]
    is_tok = (lax.broadcasted_iota(jnp.int32, (128, 128), 1) % 16) < 8
    rows = zed[:, :, :, 0:896].reshape(128, 896)
    x_slots = nn(jnp.where(is_tok, one, 0.0).astype(BF), rows).astype(BF)
    dy_slots = sum(nn(jnp.where(is_tok, 0.0, w).astype(BF), rows) for w in weights)
    dy_slots = dy_slots.astype(BF)
    sx[0] = x_slots.reshape(8, 16, 896)
    sx[1] = dy_slots.reshape(8, 16, 896)

    def window(src, dst, ss, rr):
        got = []
        for i, k in enumerate((3, -3, 2, -2, 1, -1)):
            to = (cl + k + 8) % 8
            got.append(
                go(rdma(src.at[:, to], dst(slice(None)), ss.at[i], rr.at[i], at_z(k)))
            )
        to = (cl + 4) % 8
        got.append(go(rdma(src.at[0, to], dst(0), ss.at[6], rr.at[6], at_z(4))))
        got.append(go(rdma(src.at[1, to], dst(1), ss.at[7], rr.at[7], at_z(-4))))
        return got

    got = window(sx, lambda a: xd.at[y, a, cl], b_s, b_r)
    xd[y, :, cl] = sx[:, cl]
    for q in got:
        q.wait_recv()

    left, right = (y + 3) % 4, (y + 1) % 4
    yc = {}
    for a, d in ((0, 0), (1, 1), (1, 0), (0, 1)):
        blk = xd.at[y, a]
        i = a * 2 + d
        yc[a, d] = go(rdma(blk, blk, y_s.at[i], y_r.at[i], at_y(left if d else right)))

    def half(yy):
        x = xd[yy, 0].reshape(128, 896)
        d = xd[yy, 1].reshape(128, 896)
        ps[yy, 0] = nn(x, wg_ref[0]).T.astype(BF)
        ps[yy, 1] = nn(x, wu_ref[0]).T.astype(BF)
        ps[yy, 2] = nt(d, wd_ref[0]).T.astype(BF)
        k = (yy - t + 4) % 4

        @pl.when(k != 0)
        def _():
            rdma(ps.at[yy], rp.at[t], p_s.at[k], p_r.at[k], at_x(yy)).start()

    half(y)
    yc[0, 0].wait_recv()
    blk = xd.at[left, 0]
    f0 = go(rdma(blk, blk, y_s.at[4], y_r.at[4], at_y(right)))
    yc[1, 1].wait_recv()
    blk = xd.at[right, 1]
    f1 = go(rdma(blk, blk, y_s.at[5], y_r.at[5], at_y(left)))
    yc[1, 0].wait_recv()
    half(left)
    yc[0, 1].wait_recv()
    half(right)
    f0.wait_recv()
    f1.wait_recv()
    half((y + 2) % 4)

    g = ps[t, 0].astype(F32)
    u = ps[t, 1].astype(F32)
    b = ps[t, 2].astype(F32)
    for k in (1, 3, 2):
        src = (t + 4 - k) % 4
        q = rdma(ps.at[src], rp.at[src], p_s.at[k], p_r.at[k], at_x((t + k) % 4))
        q.wait()
        g = g + rp[src, 0].astype(F32)
        u = u + rp[src, 1].astype(F32)
        b = b + rp[src, 2].astype(F32)
    s = jax.nn.sigmoid(g)
    sw = g * s
    hb[t, 0] = (sw * u).astype(BF)
    hb[t, 1] = (b * u * (s * (1.0 + g * (1.0 - s)))).astype(BF)
    hb[t, 2] = (b * sw).astype(BF)
    hc = {}
    for k in (2, 1, 3):
        blk = hb.at[t]
        hc[k] = go(rdma(blk, blk, h_s.at[k], h_r.at[k], at_x((t + k) % 4)))

    def back(j):
        os_[j, 0] = nn(flip(hb[j, 0]), wd_ref[0]).astype(BF)
        os_[j, 1] = (
            nt(flip(hb[j, 1]), wg_ref[0]) + nt(flip(hb[j, 2]), wu_ref[0])
        ).astype(BF)
        k = (j - y + 4) % 4

        @pl.when(k != 0)
        def _():
            rdma(os_.at[j], ro.at[y], o_s.at[k], o_r.at[k], at_y(j)).start()

    back(t)
    for k in (1, 3, 2):
        hc[k].wait_recv()
        back((t + 4 - k) % 4)

    for i, out in ((1, gg_ref), (2, gu_ref)):
        acc = sum(nn(hb[j, i], xd[j, 0].reshape(128, 896)) for j in range(4))
        out[0] = acc.T.astype(BF)
    acc = sum(nn(hb[j, 0], xd[j, 1].reshape(128, 896)) for j in range(4))
    gd_ref[0] = acc.astype(BF)

    acc = [os_[y, 0].astype(F32), os_[y, 1].astype(F32)]
    for k in (1, 3, 2):
        src = (y + 4 - k) % 4
        q = rdma(os_.at[src], ro.at[src], o_s.at[k], o_r.at[k], at_y((y + k) % 4))
        q.wait()
        acc = [acc[i] + ro[src, i].astype(F32) for i in range(2)]
    for i in range(2):
        sb[i] = acc[i].astype(BF).reshape(8, 16, 896)

    got = window(sb, lambda a: rb.at[a, cl], c_s, c_r)
    rb[:, cl] = sb[:, cl]
    for q in got:
        q.wait_recv()
    r0 = rb[0].reshape(128, 896)
    r1 = rb[1].reshape(128, 896)
    tot = nn(jnp.where(is_tok, 0.0, one).T.astype(BF), r1)
    for w in weights:
        tot = tot + nn(jnp.where(is_tok, w, 0.0).T.astype(BF), r0)
    ta[...] = tot.reshape(4, 2, 16, 896)
    ts[...] = ta[:, sc].astype(BF)
    q = go(rdma(ts, rs, t_s, t_r, sib))
    q.wait_recv()
    part = ta[:, c] + rs[...].astype(F32)
    ta[:, c] = part
    ts2 = part.astype(BF)
    ra[4:8] = ts2
    fc = {}
    for k in (2, 1, 3):
        fc[k] = go(
            rdma(ra.at[4 + (zh + k) % 4], ra.at[k], f_s.at[k], f_r.at[k], at_z(8 * k))
        )
    fin = ta[zh, c]
    for k in (1, 3, 2):
        fc[k].wait_recv()
        fin = fin + ra[k].astype(F32)
    fin = fin.astype(BF)
    mixed_ref[...] = fin[0:8]
    gtok_ref[...] = fin[8:16]

    for q in pend:
        q.wait_send()


def routing(expert_ids, gate_probs):
    zh = lax.axis_index("dp") // 4
    c = lax.axis_index("expert") % 2
    flat = expert_ids.reshape(16)
    earlier = jnp.arange(16)[None, :] < jnp.arange(16)[:, None]
    rank = jnp.sum((flat[:, None] == flat[None, :]) & earlier, axis=1).reshape(8, 2)
    slot = (expert_ids // 2) * 16 + zh * 4 + c * 2 + rank + 128 * (expert_ids % 2) + 1
    hi = lax.reduce_precision(gate_probs, 8, 7)
    rest = gate_probs - hi
    mid = lax.reduce_precision(rest, 8, 7)
    low = rest - mid
    table = jnp.stack(
        [slot[:, 0].astype(F32), slot[:, 1].astype(F32)]
        + [part[:, i] for i in range(2) for part in (hi, mid, low)]
    )
    table = jnp.concatenate([table, table], axis=1)
    table = jnp.pad(table, ((0, 8), (0, 0)))
    here = (jnp.arange(128) // 16) == (zh * 2 + c)
    return jnp.where(here[None, :], jnp.tile(table, (1, 8)), 0.0).astype(BF)


def shards(tokens, out_grad, expert_ids, gate_probs, w_gate, w_up, w_down):
    meta = routing(expert_ids, gate_probs)
    vm = pl.BlockSpec(memory_space=pltpu.VMEM)
    dma = pltpu.SemaphoreType.DMA
    return pl.pallas_call(
        kernel,
        out_shape=(
            jax.ShapeDtypeStruct((8, 896), BF),
            jax.ShapeDtypeStruct((8, 896), BF),
            jax.ShapeDtypeStruct((1, 896, 304), BF),
            jax.ShapeDtypeStruct((1, 896, 304), BF),
            jax.ShapeDtypeStruct((1, 304, 896), BF),
        ),
        in_specs=[vm] * 6,
        out_specs=(vm,) * 5,
        scratch_shapes=[
            pltpu.VMEM((4, 2, 16, 1024), BF),
            pltpu.VMEM((2, 8, 16, 896), BF),
            pltpu.VMEM((4, 2, 8, 16, 896), BF),
            pltpu.VMEM((4, 3, 304, 128), BF),
            pltpu.VMEM((4, 3, 304, 128), BF),
            pltpu.VMEM((4, 3, 304, 128), BF),
            pltpu.VMEM((4, 2, 128, 896), BF),
            pltpu.VMEM((4, 2, 128, 896), BF),
            pltpu.VMEM((2, 8, 16, 896), BF),
            pltpu.VMEM((2, 8, 16, 896), BF),
            pltpu.VMEM((4, 16, 896), BF),
            pltpu.VMEM((4, 16, 896), BF),
            pltpu.VMEM((4, 2, 16, 896), F32),
            pltpu.VMEM((8, 16, 896), BF),
        ]
        + [dma((4,))] * 4
        + [dma((8,))] * 4
        + [dma((4,))] * 6
        + [dma((8,))] * 2
        + [dma, dma]
        + [dma((4,))] * 2,
        compiler_params=pltpu.CompilerParams(
            collective_id=0, has_side_effects=True, vmem_limit_bytes=48 << 20
        ),
        cost_estimate=pl.CostEstimate(
            flops=2600000000, bytes_accessed=4000000, transcendentals=40000
        ),
    )(tokens, out_grad, meta, w_gate, w_up, w_down)


def solution(mesh):
    wide = P(("dp", "expert"), "tp")
    rows = P(("dp", "expert"), None)
    up = P("expert", "tp", "dp")
    down = P("expert", "dp", "tp")
    return jax.shard_map(
        shards,
        mesh=mesh,
        in_specs=(wide, wide, rows, rows, up, up, down),
        out_specs=(wide, wide, up, up, down),
        check_vma=False,
    )
```

time: 802 us -> 172 us (0.21)
  the two profiles are of different devices: /device:TPU:1 before, /device:TPU:27 now
where the time goes in v1:
time: 172 us; the launch traced here: 171 us
  Pallas kernels  161 us (94%)
  local copies, waits for them, and re-layouts  9.1 us (5%)
    pallas_call x1, Pallas kernels, shards(): pl.pallas_call(kernel, out_shape=(jax.ShapeDtypeStruct((8, 896), BF), jax...  161 us
    unnamed x18, local copies, waits for them, and re-layouts  6.64 us

profile of v1, /device:TPU:27, one launch (start us, length us, event | category | flops | bytes accessed | tf_op | source)
XLA Modules:
  0.0 171.3 jit_solution(17628483954125824962)
XLA Ops:
  0.7 0.0 copy-start.5
  0.7 0.7 copy-done.5
  1.4 0.0 copy-start.4
  1.4 0.7 copy-done.4
  2.0 0.1 copy.30
  2.1 0.1 eq.31
  2.2 0.2 convert_reduce_fusion
  2.4 0.1 reshape.55
  2.5 0.2 convert_reduce_fusion.1
  2.7 0.1 select_maximum_fusion
  2.8 0.1 tile.10
  2.9 0.0 copy-start.3
  2.9 1.5 copy.35.wg_ref
  4.4 0.0 copy-done.3
  4.4 0.0 copy-start.1
  4.4 0.0 copy-start.2
  4.4 0.4 copy.36.wu_ref
  4.8 0.3 copy-done.1
  5.1 0.0 copy-done.2
  5.2 0.0 copy-start
  5.2 1.0 copy-done
  6.2 161.0 %shard_map.110 = (bf16[8,896]{1,0:T(8,128)(2,1)S(1)}, bf16[8,896]{1,0:T(8,128)(2,1)S(1)}, bf16[1,896,304]{2,1,0:T(8,128)(2,1)S(1)}, bf16[1,896,304]{2,1,0:T(8,128)(2,1)S(1)}, bf16[1,304,896]{2,1,0:T(8,128)(2,1)S(1)}) custom-call(bf16[8,896]{1,0:T(8,128)(2,1)S(1)} %copy-done.1, bf16[8,896]{1,0:T(8,128)(2,1)S(1)} %copy-done.2, ...), custom_call_target="tpu_custom_call" | custom-call | flops 2600000000 | bytes 4000000 | tf_op jit(solution)/shard_map/pallas_call | solution.py:275
  167.2 1.1 copy.37
  168.3 1.1 copy.38
  169.3 0.6 copy.42
  169.9 0.6 copy.43
  170.5 0.8 copy.44
  (8 shorter events, 0.1 us)
Async XLA Ops:
  0.7 0.7 copy-start.5
  1.4 0.7 copy-start.4
  2.9 1.5 copy-start.3
  4.4 0.7 copy-start.1
  4.4 0.7 copy-start.2
  5.2 1.0 copy-start

commit v2 on v1

v2 whole, which is shorter than its diff:
```python
import jax
import jax.numpy as jnp
from jax import lax
from jax.experimental import pallas as pl
from jax.experimental.pallas import tpu as pltpu
from jax.sharding import PartitionSpec as P

MESH = pl.DeviceIdType.MESH
BF = jnp.bfloat16
F32 = jnp.float32


def nn(a, b):
    return lax.dot_general(a, b, (((1,), (0,)), ((), ())), preferred_element_type=F32)


def nt(a, b):
    return lax.dot_general(a, b, (((1,), (1,)), ((), ())), preferred_element_type=F32)


def tn(a, b):
    return lax.dot_general(a, b, (((0,), (0,)), ((), ())), preferred_element_type=F32)


OFFS = (4, 3, -3, 2, -2, 1, -1)


def kernel(
    tok_ref, og_ref, meta_ref, wg_ref, wu_ref, wd_ref,
    mixed_ref, gtok_ref, gg_ref, gu_ref, gd_ref,
    w, zed, sx, xd, ps, rp, hb, os_, ro, sb, rb, ts, rs, ta, ra, gr,
    a_s, a_r, s_s, s_r, b_s, b_r, y_s, y_r, v_s, v_r, p_s, p_r, h_s, h_r,
    o_s, o_r, c_s, c_r, t_s, t_r, f_s, f_r, w_m, g_m,
):
    dp = lax.axis_index("dp")
    ex = lax.axis_index("expert")
    t = lax.axis_index("tp")
    zh, y, cl, c = dp // 4, dp % 4, ex // 2, ex % 2
    z = zh * 8 + cl
    sc = 1 - c

    def at_z(k):
        zz = (z + k + 32) % 32
        return ((zz // 8) * 4 + y, (zz % 8) * 2 + c, t)

    def at_y(yy):
        return (zh * 4 + yy, ex, t)

    def at_x(tt):
        return (dp, ex, tt)

    def klass(k):
        return (cl + k + 8) % 8

    sib = (dp, cl * 2 + sc, t)

    def rdma(src, dst, ss, rr, to):
        return pltpu.make_async_remote_copy(
            src, dst, ss, rr, device_id=to, device_id_type=MESH
        )

    peers = [at_z(k) for k in (16, 8, -8, 4, -4, 3, -3, 2, -2, 1, -1)]
    peers += [at_y((y + k) % 4) for k in (1, 2, 3)]
    peers += [at_x((t + k) % 4) for k in (1, 2, 3)]
    peers += [sib]
    bar = pltpu.get_barrier_semaphore()
    for p in peers:
        pl.semaphore_signal(bar, inc=1, device_id=p, device_id_type=MESH)

    zed[zh, c, :, 0:896] = jnp.concatenate([tok_ref[...], og_ref[...]], axis=0)
    zed[zh, c, :, 896:1024] = meta_ref[...]
    loads = []
    for i, (ref, at) in enumerate(((wg_ref, 0), (wu_ref, 304), (wd_ref, 640))):
        q = pltpu.make_async_copy(ref.at[0], w.at[pl.ds(at, 304)], w_m.at[i])
        q.start()
        loads.append(q)
    w[608:640] = jnp.zeros((32, 896), BF)
    w[944:1024] = jnp.zeros((80, 896), BF)
    pl.semaphore_wait(bar, len(peers))

    pend = []

    def go(copy):
        copy.start()
        pend.append(copy)
        return copy

    ac = {}
    for k in (2, 1, 3):
        me = zed.at[zh, c]
        ac[k] = go(rdma(me, me, a_s.at[k], a_r.at[k], at_z(8 * k)))
    sc_copies = []
    for k in (0, 1, 3, 2):
        src = (zh + 4 - k) % 4
        if k:
            ac[k].wait_recv()
        blk = zed.at[src, c]
        sc_copies.append(go(rdma(blk, blk, s_s.at[k], s_r.at[k], sib)))
    for q in sc_copies:
        q.wait_recv()

    meta = jnp.zeros((16, 128), F32)
    for j in range(4):
        for cc in range(2):
            meta = meta + zed[j, cc, :, 896:1024].astype(F32)
    rid = (lax.broadcasted_iota(jnp.int32, (128, 128), 0) + 1 + 128 * c).astype(F32)
    first = rid == meta[0:1, :]
    second = rid == meta[1:2, :]
    one = jnp.where(first | second, 1.0, 0.0)
    weights = [
        jnp.where(first, meta[2 + i : 3 + i, :], 0.0)
        + jnp.where(second, meta[5 + i : 6 + i, :], 0.0)
        for i in range(3)
    ]
    is_tok = (lax.broadcasted_iota(jnp.int32, (128, 128), 1) % 16) < 8
    rows = zed[:, :, :, 0:896].reshape(128, 896)
    x_slots = nn(jnp.where(is_tok, one, 0.0).astype(BF), rows).astype(BF)
    dy_slots = sum(nn(jnp.where(is_tok, 0.0, m).astype(BF), rows) for m in weights)
    dy_slots = dy_slots.astype(BF)
    sx[0] = x_slots.reshape(8, 16, 896)
    sx[1] = dy_slots.reshape(8, 16, 896)

    def near(src, dst, ss, rr, i):
        k = OFFS[i]
        to = klass(k)
        if i:
            return [go(rdma(src.at[:, to], dst(slice(None)), ss.at[i], rr.at[i], at_z(k)))]
        return [
            go(rdma(src.at[0, to], dst(0), ss.at[0], rr.at[0], at_z(4))),
            go(rdma(src.at[1, to], dst(1), ss.at[7], rr.at[7], at_z(-4))),
        ]

    got = {i: near(sx, lambda a: xd.at[y, a, cl], b_s, b_r, i) for i in range(7)}
    xd[y, :, cl] = sx[:, cl]

    left, right = (y + 3) % 4, (y + 1) % 4
    yc = []
    for i in (7, 5, 6, 3, 4, 1, 2, 0):
        src = cl if i == 7 else klass(-OFFS[i])
        if i < 7:
            for q in got[i]:
                q.wait_recv()
        blk = xd.at[y, :, src]
        yc.append(
            (
                src,
                i,
                go(rdma(blk, blk, y_s.at[0, i], y_r.at[0, i], at_y(right))),
                go(rdma(blk, blk, y_s.at[1, i], y_r.at[1, i], at_y(left))),
            )
        )
    for q in loads:
        q.wait()

    chunks = (y, left, right, (y + 2) % 4)

    def half(m):
        yy = chunks[m]
        gu = nt(xd[yy, 0].reshape(128, 896), w[0:640])
        b = nt(xd[yy, 1].reshape(128, 896), w[640:1024])
        ps[m, :, :, 0:640] = gu.astype(BF).reshape(4, 32, 640)
        ps[m, :, :, 640:1024] = b.astype(BF).reshape(4, 32, 384)
        for k in (2, 1, 3):
            q = (t + k) % 4
            go(rdma(ps.at[m, q], rp.at[m, k], p_s.at[m, k], p_r.at[m, k], at_x(q)))

    def middle(m):
        acc = ps[m, t].astype(F32)
        for k in (1, 3, 2):
            ref = rp.at[m, k]
            rdma(ref, ref, p_s.at[m, k], p_r.at[m, k], at_x((t + k) % 4)).wait_recv()
            acc = acc + rp[m, k].astype(F32)
        g, u, b = acc[:, 0:304], acc[:, 304:608], acc[:, 640:944]
        s = jax.nn.sigmoid(g)
        sw = g * s
        hb[m, t] = jnp.concatenate(
            [
                b * u * (s * (1.0 + g * (1.0 - s))),
                b * sw,
                jnp.zeros((32, 32), F32),
                sw * u,
                jnp.zeros((32, 80), F32),
            ],
            axis=1,
        ).astype(BF)
        for k in (2, 1, 3):
            blk = hb.at[m, t]
            go(rdma(blk, blk, h_s.at[m, k], h_r.at[m, k], at_x((t + k) % 4)))

    def back(m):
        for k in (1, 3, 2):
            blk = hb.at[m, (t + 4 - k) % 4]
            rdma(blk, blk, h_s.at[m, k], h_r.at[m, k], at_x((t + k) % 4)).wait_recv()
        h = hb[m].reshape(128, 1024)
        os_[m, 0] = nn(h[:, 640:1024], w[640:1024]).astype(BF).reshape(8, 16, 896)
        os_[m, 1] = nn(h[:, 0:640], w[0:640]).astype(BF).reshape(8, 16, 896)
        if m:
            for i in range(8):
                to = cl if i == 7 else klass(OFFS[i])
                go(
                    rdma(
                        os_.at[m, :, to], ro.at[m, :, to],
                        o_s.at[m, i], o_r.at[m, i], at_y(chunks[m]),
                    )
                )

    half(0)
    fw = []
    for src, i, to_right, to_left in yc:
        to_right.wait_recv()
        blk = xd.at[left, 0, src]
        fw.append(go(rdma(blk, blk, v_s.at[0, i], v_r.at[0, i], at_y(right))))
        to_left.wait_recv()
        blk = xd.at[right, 1, src]
        fw.append(go(rdma(blk, blk, v_s.at[1, i], v_r.at[1, i], at_y(left))))
    half(1)
    half(2)
    middle(0)
    for q in fw:
        q.wait_recv()
    half(3)
    middle(1)
    middle(2)
    back(0)
    back(1)
    back(2)
    middle(3)
    back(3)

    order = [xd[chunks[m], 0].reshape(128, 896) for m in range(4)]
    xs = jnp.concatenate(order, axis=0)
    ds = jnp.concatenate([xd[chunks[m], 1].reshape(128, 896) for m in range(4)], axis=0)
    hs = hb[...].reshape(512, 1024)
    for at, n, r in ((0, 256, xs), (256, 256, xs), (512, 128, xs), (640, 384, ds)):
        gr[at : at + n] = tn(hs[:, at : at + n], r).astype(BF)
    saves = []
    for i, (ref, at) in enumerate(((gg_ref, 0), (gu_ref, 304), (gd_ref, 640))):
        q = pltpu.make_async_copy(gr.at[pl.ds(at, 304)], ref.at[0], g_m.at[i])
        q.start()
        saves.append(q)

    got = []
    for i in range(8):
        to = cl if i == 7 else klass(OFFS[i])
        acc = os_[0, :, to].astype(F32)
        for m in (1, 2, 3):
            ref = ro.at[m, :, to]
            rdma(ref, ref, o_s.at[m, i], o_r.at[m, i], at_y(chunks[m])).wait_recv()
            acc = acc + ro[m, :, to].astype(F32)
        if i == 7:
            rb[:, cl] = acc.astype(BF)
        else:
            sb[:, to] = acc.astype(BF)
            got += near(sb, lambda a: rb.at[a, cl], c_s, c_r, i)
    for q in got:
        q.wait_recv()

    r0 = rb[0].reshape(128, 896)
    r1 = rb[1].reshape(128, 896)
    tot = nn(jnp.where(is_tok, 0.0, one).T.astype(BF), r1)
    for m in weights:
        tot = tot + nn(jnp.where(is_tok, m, 0.0).T.astype(BF), r0)
    ta[...] = tot.reshape(4, 2, 16, 896)
    ts[...] = ta[:, sc].astype(BF)
    go(rdma(ts, rs, t_s, t_r, sib)).wait_recv()
    part = ta[:, c] + rs[...].astype(F32)
    ta[:, c] = part
    ra[4:8] = part.astype(BF)
    fc = {}
    for k in (2, 1, 3):
        fc[k] = go(
            rdma(ra.at[4 + (zh + k) % 4], ra.at[k], f_s.at[k], f_r.at[k], at_z(8 * k))
        )
    fin = ta[zh, c]
    for k in (1, 3, 2):
        fc[k].wait_recv()
        fin = fin + ra[k].astype(F32)
    fin = fin.astype(BF)
    mixed_ref[...] = fin[0:8]
    gtok_ref[...] = fin[8:16]

    for q in pend:
        q.wait_send()
    for q in saves:
        q.wait()


def routing(expert_ids, gate_probs):
    zh = lax.axis_index("dp") // 4
    c = lax.axis_index("expert") % 2
    flat = expert_ids.reshape(16)
    earlier = jnp.arange(16)[None, :] < jnp.arange(16)[:, None]
    rank = jnp.sum((flat[:, None] == flat[None, :]) & earlier, axis=1).reshape(8, 2)
    slot = (expert_ids // 2) * 16 + zh * 4 + c * 2 + rank + 128 * (expert_ids % 2) + 1
    hi = lax.reduce_precision(gate_probs, 8, 7)
    rest = gate_probs - hi
    mid = lax.reduce_precision(rest, 8, 7)
    low = rest - mid
    table = jnp.stack(
        [slot[:, 0].astype(F32), slot[:, 1].astype(F32)]
        + [part[:, i] for i in range(2) for part in (hi, mid, low)]
    )
    table = jnp.concatenate([table, table], axis=1)
    table = jnp.pad(table, ((0, 8), (0, 0)))
    here = (jnp.arange(128) // 16) == (zh * 2 + c)
    return jnp.where(here[None, :], jnp.tile(table, (1, 8)), 0.0).astype(BF)


def shards(tokens, out_grad, expert_ids, gate_probs, w_gate, w_up, w_down):
    meta = routing(expert_ids, gate_probs)
    vm = pl.BlockSpec(memory_space=pltpu.VMEM)
    hbm = pl.BlockSpec(memory_space=pl.ANY)
    dma = pltpu.SemaphoreType.DMA
    mixed, gtok, gg, gu, gd = pl.pallas_call(
        kernel,
        out_shape=(
            jax.ShapeDtypeStruct((8, 896), BF),
            jax.ShapeDtypeStruct((8, 896), BF),
            jax.ShapeDtypeStruct((1, 304, 896), BF),
            jax.ShapeDtypeStruct((1, 304, 896), BF),
            jax.ShapeDtypeStruct((1, 304, 896), BF),
        ),
        in_specs=[vm] * 3 + [hbm] * 3,
        out_specs=(vm,) * 2 + (hbm,) * 3,
        scratch_shapes=[
            pltpu.VMEM((1024, 896), BF),
            pltpu.VMEM((4, 2, 16, 1024), BF),
            pltpu.VMEM((2, 8, 16, 896), BF),
            pltpu.VMEM((4, 2, 8, 16, 896), BF),
            pltpu.VMEM((4, 4, 32, 1024), BF),
            pltpu.VMEM((4, 4, 32, 1024), BF),
            pltpu.VMEM((4, 4, 32, 1024), BF),
            pltpu.VMEM((4, 2, 8, 16, 896), BF),
            pltpu.VMEM((4, 2, 8, 16, 896), BF),
            pltpu.VMEM((2, 8, 16, 896), BF),
            pltpu.VMEM((2, 8, 16, 896), BF),
            pltpu.VMEM((4, 16, 896), BF),
            pltpu.VMEM((4, 16, 896), BF),
            pltpu.VMEM((4, 2, 16, 896), F32),
            pltpu.VMEM((8, 16, 896), BF),
            pltpu.VMEM((1024, 896), BF),
        ]
        + [dma((4,))] * 4
        + [dma((8,))] * 2
        + [dma((2, 8))] * 4
        + [dma((4, 4))] * 4
        + [dma((4, 8))] * 2
        + [dma((8,))] * 2
        + [dma, dma]
        + [dma((4,))] * 2
        + [dma((3,))] * 2,
        compiler_params=pltpu.CompilerParams(
            collective_id=0, has_side_effects=True, vmem_limit_bytes=48 << 20
        ),
        cost_estimate=pl.CostEstimate(
            flops=2600000000, bytes_accessed=4000000, transcendentals=40000
        ),
    )(
        tokens, out_grad, meta,
        w_gate.transpose(0, 2, 1), w_up.transpose(0, 2, 1), w_down,
    )
    return mixed, gtok, gg.transpose(0, 2, 1), gu.transpose(0, 2, 1), gd


def solution(mesh):
    wide = P(("dp", "expert"), "tp")
    rows = P(("dp", "expert"), None)
    up = P("expert", "tp", "dp")
    down = P("expert", "dp", "tp")
    return jax.shard_map(
        shards,
        mesh=mesh,
        in_specs=(wide, wide, rows, rows, up, up, down),
        out_specs=(wide, wide, up, up, down),
        check_vma=False,
    )
```

time: 172 us -> 150 us (0.87)
  the two profiles are of different devices: /device:TPU:27 before, /device:TPU:1 now
where the time goes in v2:
time: 150 us
  Pallas kernels  140 us (93%)
  local copies, waits for them, and re-layouts  9.11 us (6%)
    pallas_call x1, Pallas kernels, shards(): pl.pallas_call(kernel, out_shape=(jax.ShapeDtypeStruct((8, 896), BF), jax...  140 us
    unnamed x20, local copies, waits for them, and re-layouts  8.79 us

profile of v2, /device:TPU:1, one launch (start us, length us, event | category | flops | bytes accessed | tf_op | source)
XLA Modules:
  0.0 149.8 jit_solution(6155723039001253409)
XLA Ops:
  0.7 0.0 copy-start.6
  0.7 0.7 copy-done.6
  1.4 0.0 copy-start.5
  1.4 0.7 copy-done.5
  2.1 0.1 copy.22
  2.1 0.1 eq.31
  2.2 0.2 convert_reduce_fusion
  2.4 0.1 reshape.55
  2.5 0.2 convert_reduce_fusion.1
  2.7 0.1 select_maximum_fusion
  2.8 0.0 copy-start.3
  2.8 0.0 copy-start.4
  2.9 0.1 tile.10
  3.0 0.6 copy-done.3
  3.5 0.0 copy-done.4
  3.6 0.0 copy-start
  3.6 1.0 copy-done
  4.6 0.0 copy-start.1
  4.6 1.0 copy-done.1
  5.7 0.0 copy-start.2
  5.7 1.0 copy-done.2
  6.7 139.5 %shard_map.110 = (bf16[8,896]{1,0:T(8,128)(2,1)S(1)}, bf16[8,896]{1,0:T(8,128)(2,1)S(1)}, bf16[1,304,896]{2,1,0:T(8,128)(2,1)S(1)}, bf16[1,304,896]{2,1,0:T(8,128)(2,1)S(1)}, bf16[1,304,896]{2,1,0:T(8,128)(2,1)S(1)}) custom-call(bf16[8,896]{1,0:T(8,128)(2,1)S(1)} %copy-done.3, bf16[8,896]{1,0:T(8,128)(2,1)S(1)} %copy-done.4, ...), custom_call_target="tpu_custom_call" | custom-call | flops 2600000000 | bytes 4000000 | tf_op jit(solution)/shard_map/pallas_call | solution.py:314
  146.2 0.6 copy.32
  146.8 0.6 copy.33
  147.4 0.8 copy.34
  148.2 0.8 copy.35
  149.0 0.8 copy.36
  (8 shorter events, 0.1 us)
Async XLA Ops:
  0.7 0.7 copy-start.6
  1.4 0.7 copy-start.5
  2.8 0.7 copy-start.3
  2.8 0.7 copy-start.4
  3.6 1.0 copy-start
  4.6 1.0 copy-start.1
  5.7 1.0 copy-start.2

commit v3 on v2

--- a/solution.py
+++ b/solution.py
@@ -25,12 +25,31 @@
 OFFS = (4, 3, -3, 2, -2, 1, -1)
 
 
+def routing(ids, probs, zh, c):
+    rank = jnp.zeros((2, 8), jnp.int32)
+    for d in range(1, 8):
+        before = jnp.concatenate([jnp.full((2, d), -1, jnp.int32), ids[:, : 8 - d]], axis=1)
+        same = (ids == before[0:1]) | (ids == before[1:2])
+        rank = rank + jnp.where(same, 1, 0)
+    slot = (ids >> 1) * 16 + (ids & 1) * 128 + rank + (zh * 4 + c * 2 + 1)
+    slot = slot.astype(F32)
+    hi = probs.astype(BF).astype(F32)
+    mid = (probs - hi).astype(BF).astype(F32)
+    low = probs - hi - mid
+    table = [slot] + [part[i : i + 1] for i in range(2) for part in (hi, mid, low)]
+    table = jnp.concatenate(table, axis=0)
+    table = jnp.concatenate([table] * 16, axis=1)
+    here = (lax.broadcasted_iota(jnp.int32, (8, 128), 1) // 16) == (zh * 2 + c)
+    table = jnp.where(here, table, 0.0)
+    return jnp.concatenate([table, jnp.zeros((8, 128), F32)], axis=0).astype(BF)
+
+
 def kernel(
-    tok_ref, og_ref, meta_ref, wg_ref, wu_ref, wd_ref,
+    tok_ref, og_ref, ids_ref, probs_ref, wg_ref, wu_ref, wd_ref,
     mixed_ref, gtok_ref, gg_ref, gu_ref, gd_ref,
-    w, zed, sx, xd, ps, rp, hb, os_, ro, sb, rb, ts, rs, ta, ra, gr,
+    w, zed, sx, xd, ps, rp, hb, os_, ro, sb, rb, ts, rs, fs, f1, fg, f2, gr,
     a_s, a_r, s_s, s_r, b_s, b_r, y_s, y_r, v_s, v_r, p_s, p_r, h_s, h_r,
-    o_s, o_r, c_s, c_r, t_s, t_r, f_s, f_r, w_m, g_m,
+    o_s, o_r, c_s, c_r, t_s, t_r, f_s, f_r, w_m,
 ):
     dp = lax.axis_index("dp")
     ex = lax.axis_index("expert")
@@ -59,7 +78,7 @@
             src, dst, ss, rr, device_id=to, device_id_type=MESH
         )
 
-    peers = [at_z(k) for k in (16, 8, -8, 4, -4, 3, -3, 2, -2, 1, -1)]
+    peers = [at_z(k) for k in (8, -8, 4, -4, 3, -3, 2, -2, 1, -1)]
     peers += [at_y((y + k) % 4) for k in (1, 2, 3)]
     peers += [at_x((t + k) % 4) for k in (1, 2, 3)]
     peers += [sib]
@@ -68,7 +87,7 @@
         pl.semaphore_signal(bar, inc=1, device_id=p, device_id_type=MESH)
 
     zed[zh, c, :, 0:896] = jnp.concatenate([tok_ref[...], og_ref[...]], axis=0)
-    zed[zh, c, :, 896:1024] = meta_ref[...]
+    zed[zh, c, :, 896:1024] = routing(ids_ref[...], probs_ref[...], zh, c)
     loads = []
     for i, (ref, at) in enumerate(((wg_ref, 0), (wu_ref, 304), (wd_ref, 640))):
         q = pltpu.make_async_copy(ref.at[0], w.at[pl.ds(at, 304)], w_m.at[i])
@@ -85,17 +104,34 @@
         pend.append(copy)
         return copy
 
-    ac = {}
-    for k in (2, 1, 3):
-        me = zed.at[zh, c]
-        ac[k] = go(rdma(me, me, a_s.at[k], a_r.at[k], at_z(8 * k)))
+    up, down = at_z(8), at_z(-8)
+    zr, zl, zo = (zh + 1) % 4, (zh + 3) % 4, (zh + 2) % 4
+    halves = (pl.ds(0, 512), pl.ds(512, 512))
+
+    def along(who, h, i, to):
+        blk = zed.at[who, c, :, halves[h]]
+        return go(rdma(blk, blk, a_s.at[i], a_r.at[i], to))
+
+    ac = [along(zh, i // 2 ^ i % 2, i, (up, down)[i % 2]) for i in range(4)]
     sc_copies = []
-    for k in (0, 1, 3, 2):
-        src = (zh + 4 - k) % 4
-        if k:
-            ac[k].wait_recv()
-        blk = zed.at[src, c]
-        sc_copies.append(go(rdma(blk, blk, s_s.at[k], s_r.at[k], sib)))
+
+    def across(who):
+        blk = zed.at[who, c]
+        i = len(sc_copies)
+        sc_copies.append(go(rdma(blk, blk, s_s.at[i], s_r.at[i], sib)))
+
+    across(zh)
+    ac[0].wait_recv()
+    ac.append(along(zl, 0, 4, up))
+    ac[1].wait_recv()
+    ac.append(along(zr, 1, 5, down))
+    ac[2].wait_recv()
+    across(zl)
+    ac[3].wait_recv()
+    across(zr)
+    ac[4].wait_recv()
+    ac[5].wait_recv()
+    across(zo)
     for q in sc_copies:
         q.wait_recv()
 
@@ -192,15 +228,14 @@
             blk = hb.at[m, (t + 4 - k) % 4]
             rdma(blk, blk, h_s.at[m, k], h_r.at[m, k], at_x((t + k) % 4)).wait_recv()
         h = hb[m].reshape(128, 1024)
-        os_[m, 0] = nn(h[:, 640:1024], w[640:1024]).astype(BF).reshape(8, 16, 896)
-        os_[m, 1] = nn(h[:, 0:640], w[0:640]).astype(BF).reshape(8, 16, 896)
-        if m:
-            for i in range(8):
+        for a, lo, hi in ((0, 640, 1024), (1, 0, 640)):
+            os_[m, a] = nn(h[:, lo:hi], w[lo:hi]).astype(BF).reshape(8, 16, 896)
+            for i in range(8 if m else 0):
                 to = cl if i == 7 else klass(OFFS[i])
                 go(
                     rdma(
-                        os_.at[m, :, to], ro.at[m, :, to],
-                        o_s.at[m, i], o_r.at[m, i], at_y(chunks[m]),
+                        os_.at[m, a, to], ro.at[m, a, to],
+                        o_s.at[m, a, i], o_r.at[m, a, i], at_y(chunks[m]),
                     )
                 )
 
@@ -233,83 +268,92 @@
     hs = hb[...].reshape(512, 1024)
     for at, n, r in ((0, 256, xs), (256, 256, xs), (512, 128, xs), (640, 384, ds)):
         gr[at : at + n] = tn(hs[:, at : at + n], r).astype(BF)
-    saves = []
-    for i, (ref, at) in enumerate(((gg_ref, 0), (gu_ref, 304), (gd_ref, 640))):
-        q = pltpu.make_async_copy(gr.at[pl.ds(at, 304)], ref.at[0], g_m.at[i])
-        q.start()
-        saves.append(q)
-
-    got = []
-    for i in range(8):
-        to = cl if i == 7 else klass(OFFS[i])
-        acc = os_[0, :, to].astype(F32)
-        for m in (1, 2, 3):
-            ref = ro.at[m, :, to]
-            rdma(ref, ref, o_s.at[m, i], o_r.at[m, i], at_y(chunks[m])).wait_recv()
-            acc = acc + ro[m, :, to].astype(F32)
-        if i == 7:
-            rb[:, cl] = acc.astype(BF)
-        else:
-            sb[:, to] = acc.astype(BF)
-            got += near(sb, lambda a: rb.at[a, cl], c_s, c_r, i)
-    for q in got:
-        q.wait_recv()
-
-    r0 = rb[0].reshape(128, 896)
-    r1 = rb[1].reshape(128, 896)
-    tot = nn(jnp.where(is_tok, 0.0, one).T.astype(BF), r1)
-    for m in weights:
-        tot = tot + nn(jnp.where(is_tok, m, 0.0).T.astype(BF), r0)
-    ta[...] = tot.reshape(4, 2, 16, 896)
-    ts[...] = ta[:, sc].astype(BF)
-    go(rdma(ts, rs, t_s, t_r, sib)).wait_recv()
-    part = ta[:, c] + rs[...].astype(F32)
-    ta[:, c] = part
-    ra[4:8] = part.astype(BF)
-    fc = {}
-    for k in (2, 1, 3):
-        fc[k] = go(
-            rdma(ra.at[4 + (zh + k) % 4], ra.at[k], f_s.at[k], f_r.at[k], at_z(8 * k))
-        )
-    fin = ta[zh, c]
-    for k in (1, 3, 2):
-        fc[k].wait_recv()
-        fin = fin + ra[k].astype(F32)
-    fin = fin.astype(BF)
-    mixed_ref[...] = fin[0:8]
-    gtok_ref[...] = fin[8:16]
+    gg_ref[0], gu_ref[0], gd_ref[0] = gr[0:304], gr[304:608], gr[640:944]
+
+    def gather(a):
+        got = []
+        for i in range(8):
+            k = 0 if i == 7 else OFFS[i]
+            to = klass(k)
+            acc = os_[0, a, to].astype(F32)
+            for m in (1, 2, 3):
+                ref = ro.at[m, a, to]
+                rdma(
+                    ref, ref, o_s.at[m, a, i], o_r.at[m, a, i], at_y(chunks[m])
+                ).wait_recv()
+                acc = acc + ro[m, a, to].astype(F32)
+            if i == 7:
+                rb[a, cl] = acc.astype(BF)
+            else:
+                sb[a, to] = acc.astype(BF)
+                dest = at_z(-4 if i == 0 and a else k)
+                got.append(
+                    go(rdma(sb.at[a, to], rb.at[a, cl], c_s.at[a, i], c_r.at[a, i], dest))
+                )
+        return got
+
+    def combine(a, got):
+        for q in got:
+            q.wait_recv()
+        r = rb[a].reshape(128, 896)
+        tot = sum(nn(m.T.astype(BF), r) for m in ([one] if a else weights))
+        tot = tot.reshape(4, 2, 2, 8, 896)
+        sides = (tot[:, 0, 0], tot[:, 1, 0])
+        mine = jnp.where(c == 0, sides[0], sides[1])
+        other = jnp.where(c == 0, sides[1], sides[0])
+        ts[a] = other.reshape(32, 896).astype(BF)
+        go(rdma(ts.at[a], rs.at[a], t_s.at[a], t_r.at[a], sib)).wait_recv()
+        mine = mine + rs[a].reshape(4, 8, 896).astype(F32)
+        tail = jnp.concatenate([mine[:, :, 512:896], jnp.zeros((4, 8, 128), F32)], axis=2)
+        fs[a] = jnp.concatenate([mine[:, :, 0:512], tail], axis=1)
+        fg[a, 0] = fs[a, zo].astype(BF)
+        fg[a, 1, :, 256:512] = fs[a, zr, :, 256:512].astype(BF)
+        fg[a, 2, :, 0:256] = fs[a, zl, :, 0:256].astype(BF)
+        lo, hi = pl.ds(0, 256), pl.ds(256, 256)
+
+        def hop(src, dst, i, to):
+            return go(rdma(src, dst, f_s.at[a, i], f_r.at[a, i], to))
+
+        return [
+            hop(fg.at[a, 0, :, lo], f1.at[a, 0], 0, up),
+            hop(fg.at[a, 0, :, hi], f1.at[a, 1], 1, down),
+            hop(fg.at[a, 1, :, hi], f2.at[a, 0, :, hi], 2, up),
+            hop(fg.at[a, 2, :, lo], f2.at[a, 1, :, lo], 3, down),
+        ]
+
+    def relay(a, hops):
+        lo, hi = pl.ds(0, 256), pl.ds(256, 256)
+        hops[0].wait_recv()
+        fg[a, 1, :, 0:256] = (fs[a, zr, :, 0:256] + f1[a, 0].astype(F32)).astype(BF)
+        q = rdma(fg.at[a, 1, :, lo], f2.at[a, 0, :, lo], f_s.at[a, 4], f_r.at[a, 4], up)
+        hops.append(go(q))
+        hops[1].wait_recv()
+        fg[a, 2, :, 256:512] = (fs[a, zl, :, 256:512] + f1[a, 1].astype(F32)).astype(BF)
+        q = rdma(fg.at[a, 2, :, hi], f2.at[a, 1, :, hi], f_s.at[a, 5], f_r.at[a, 5], down)
+        hops.append(go(q))
+
+    def finish(a, hops, ref):
+        for q in hops[2:]:
+            q.wait_recv()
+        fin = fs[a, zh] + f2[a, 0].astype(F32) + f2[a, 1].astype(F32)
+        ref[:, 0:512] = fin[0:8].astype(BF)
+        ref[:, 512:896] = fin[8:16, 0:384].astype(BF)
+
+    hops0 = combine(0, gather(0))
+    got = gather(1)
+    relay(0, hops0)
+    hops1 = combine(1, got)
+    relay(1, hops1)
+    finish(0, hops0, mixed_ref)
+    finish(1, hops1, gtok_ref)
 
     for q in pend:
         q.wait_send()
-    for q in saves:
-        q.wait()
-
-
-def routing(expert_ids, gate_probs):
-    zh = lax.axis_index("dp") // 4
-    c = lax.axis_index("expert") % 2
-    flat = expert_ids.reshape(16)
-    earlier = jnp.arange(16)[None, :] < jnp.arange(16)[:, None]
-    rank = jnp.sum((flat[:, None] == flat[None, :]) & earlier, axis=1).reshape(8, 2)
-    slot = (expert_ids // 2) * 16 + zh * 4 + c * 2 + rank + 128 * (expert_ids % 2) + 1
-    hi = lax.reduce_precision(gate_probs, 8, 7)
-    rest = gate_probs - hi
-    mid = lax.reduce_precision(rest, 8, 7)
-    low = rest - mid
-    table = jnp.stack(
-        [slot[:, 0].astype(F32), slot[:, 1].astype(F32)]
-        + [part[:, i] for i in range(2) for part in (hi, mid, low)]
-    )
-    table = jnp.concatenate([table, table], axis=1)
-    table = jnp.pad(table, ((0, 8), (0, 0)))
-    here = (jnp.arange(128) // 16) == (zh * 2 + c)
-    return jnp.where(here[None, :], jnp.tile(table, (1, 8)), 0.0).astype(BF)
 
 
 def shards(tokens, out_grad, expert_ids, gate_probs, w_gate, w_up, w_down):
-    meta = routing(expert_ids, gate_probs)
     vm = pl.BlockSpec(memory_space=pltpu.VMEM)
-    hbm = pl.BlockSpec(memory_space=pl.ANY)
+    hbm = pl.BlockSpec(memory_space=pltpu.HBM)
     dma = pltpu.SemaphoreType.DMA
     mixed, gtok, gg, gu, gd = pl.pallas_call(
         kernel,
@@ -320,8 +364,8 @@
             jax.ShapeDtypeStruct((1, 304, 896), BF),
             jax.ShapeDtypeStruct((1, 304, 896), BF),
         ),
-        in_specs=[vm] * 3 + [hbm] * 3,
-        out_specs=(vm,) * 2 + (hbm,) * 3,
+        in_specs=[vm] * 4 + [hbm] * 3,
+        out_specs=(vm,) * 5,
         scratch_shapes=[
             pltpu.VMEM((1024, 896), BF),
             pltpu.VMEM((4, 2, 16, 1024), BF),
@@ -334,29 +378,32 @@
             pltpu.VMEM((4, 2, 8, 16, 896), BF),
             pltpu.VMEM((2, 8, 16, 896), BF),
             pltpu.VMEM((2, 8, 16, 896), BF),
-            pltpu.VMEM((4, 16, 896), BF),
-            pltpu.VMEM((4, 16, 896), BF),
-            pltpu.VMEM((4, 2, 16, 896), F32),
-            pltpu.VMEM((8, 16, 896), BF),
+            pltpu.VMEM((2, 32, 896), BF),
+            pltpu.VMEM((2, 32, 896), BF),
+            pltpu.VMEM((2, 4, 16, 512), F32),
+            pltpu.VMEM((2, 2, 16, 256), BF),
+            pltpu.VMEM((2, 3, 16, 512), BF),
+            pltpu.VMEM((2, 2, 16, 512), BF),
             pltpu.VMEM((1024, 896), BF),
         ]
-        + [dma((4,))] * 4
+        + [dma((6,))] * 2
+        + [dma((4,))] * 2
         + [dma((8,))] * 2
         + [dma((2, 8))] * 4
         + [dma((4, 4))] * 4
-        + [dma((4, 8))] * 2
-        + [dma((8,))] * 2
-        + [dma, dma]
-        + [dma((4,))] * 2
-        + [dma((3,))] * 2,
+        + [dma((4, 2, 8))] * 2
+        + [dma((2, 7))] * 2
+        + [dma((2,))] * 2
+        + [dma((2, 6))] * 2
+        + [dma((3,))],
         compiler_params=pltpu.CompilerParams(
-            collective_id=0, has_side_effects=True, vmem_limit_bytes=48 << 20
+            collective_id=0, has_side_effects=True, vmem_limit_bytes=60 << 20
         ),
         cost_estimate=pl.CostEstimate(
             flops=2600000000, bytes_accessed=4000000, transcendentals=40000
         ),
     )(
-        tokens, out_grad, meta,
+        tokens, out_grad, expert_ids.T, gate_probs.T,
         w_gate.transpose(0, 2, 1), w_up.transpose(0, 2, 1), w_down,
     )
     return mixed, gtok, gg.transpose(0, 2, 1), gu.transpose(0, 2, 1), gd

time: 150 us -> 145 us (0.967)
  local copies, waits for them, and re-layouts: 9.11 us -> 5.92 us
  Pallas kernels: 140 us -> 138 us
    unnamed x20 -> x11, local copies, waits for them, and re-layouts: 8.79 us -> 5.92 us
    pallas_call x1, Pallas kernels: 140 us -> 138 us  [shards(): pl.pallas_call(kernel, out_shape=(jax.ShapeDtypeStruct((8, 896), BF), jax...]
where the time goes in v3:
time: 145 us; the launch traced here: 144 us
  Pallas kernels  138 us (95%)
  local copies, waits for them, and re-layouts  5.92 us (4%)
    pallas_call x1, Pallas kernels, shards(): pl.pallas_call(kernel, out_shape=(jax.ShapeDtypeStruct((8, 896), BF), jax...  138 us
    unnamed x11, local copies, waits for them, and re-layouts  5.92 us

profile of v3, /device:TPU:1, one launch (start us, length us, event | category | flops | bytes accessed | tf_op | source)
XLA Modules:
  0.0 144.3 jit_solution(18030818817596690588)
XLA Ops:
  0.6 137.7 %shard_map.110 = (bf16[8,896]{1,0:T(8,128)(2,1)}, bf16[8,896]{1,0:T(8,128)(2,1)}, bf16[1,304,896]{2,1,0:T(8,128)(2,1)}, bf16[1,304,896]{2,1,0:T(8,128)(2,1)}, bf16[1,304,896]{2,1,0:T(8,128)(2,1)}) custom-call(bf16[8,896]{1,0:T(8,128)(2,1)} %tok_ref.1, bf16[8,896]{1,0:T(8,128)(2,1)} %og_ref.1, s32[2,8]{1,0:T(2,128)} %bitcast.10, f32[2,8]{1,0:T(2,128)} %bitcast.11, ...), custom_call_target="tpu_custom_call" | custom-call | flops 2600000000 | bytes 4000000 | tf_op jit(solution)/shard_map/pallas_call | solution.py:358
  138.4 0.0 copy-start.2
  138.4 1.3 copy.17
  139.7 0.0 copy-done.2
  139.7 0.6 copy.18
  140.3 0.0 copy-start.1
  140.3 2.0 %copy.19 = bf16[1,896,304]{1,2,0:T(8,128)(2,1)} copy(bf16[1,896,304]{1,2,0:T(8,128)(2,1)} %bitcast.7) | data formatting | bytes 1089536
  142.2 0.0 copy-done.1
  142.2 0.0 copy-start
  142.3 0.8 copy.20
  143.1 0.4 copy-done
  143.5 0.8 copy.21
Async XLA Ops:
  138.4 1.3 copy-start.2
  140.3 2.0 %copy-start.1 = (bf16[1,304,896]{2,1,0:T(8,128)(2,1)S(1)}, bf16[1,304,896]{2,1,0:T(8,128)(2,1)}, u32[]{:S(2)}) copy-start(bf16[1,304,896]{2,1,0:T(8,128)(2,1)} %get-tuple-element.13) | copy-start | bytes 1634308
  142.2 1.2 copy-start

commit v4 on v3

--- a/solution.py
+++ b/solution.py
@@ -46,8 +46,8 @@
 
 def kernel(
     tok_ref, og_ref, ids_ref, probs_ref, wg_ref, wu_ref, wd_ref,
-    mixed_ref, gtok_ref, gg_ref, gu_ref, gd_ref,
-    w, zed, sx, xd, ps, rp, hb, os_, ro, sb, rb, ts, rs, fs, f1, fg, f2, gr,
+    fin_ref, gr,
+    w, zed, sx, xd, ps, rp, hb, os_, ro, sb, rb, ts, rs, fs, f1, fg, f2,
     a_s, a_r, s_s, s_r, b_s, b_r, y_s, y_r, v_s, v_r, p_s, p_r, h_s, h_r,
     o_s, o_r, c_s, c_r, t_s, t_r, f_s, f_r, w_m,
 ):
@@ -251,16 +251,16 @@
     half(1)
     half(2)
     middle(0)
+    middle(1)
+    middle(2)
+    back(1)
+    back(2)
     for q in fw:
         q.wait_recv()
     half(3)
-    middle(1)
-    middle(2)
-    back(0)
-    back(1)
-    back(2)
     middle(3)
     back(3)
+    back(0)
 
     order = [xd[chunks[m], 0].reshape(128, 896) for m in range(4)]
     xs = jnp.concatenate(order, axis=0)
@@ -268,8 +268,6 @@
     hs = hb[...].reshape(512, 1024)
     for at, n, r in ((0, 256, xs), (256, 256, xs), (512, 128, xs), (640, 384, ds)):
         gr[at : at + n] = tn(hs[:, at : at + n], r).astype(BF)
-    gg_ref[0], gu_ref[0], gd_ref[0] = gr[0:304], gr[304:608], gr[640:944]
-
     def gather(a):
         got = []
         for i in range(8):
@@ -332,40 +330,48 @@
         q = rdma(fg.at[a, 2, :, hi], f2.at[a, 1, :, hi], f_s.at[a, 5], f_r.at[a, 5], down)
         hops.append(go(q))
 
-    def finish(a, hops, ref):
+    def finish(a, hops):
         for q in hops[2:]:
             q.wait_recv()
         fin = fs[a, zh] + f2[a, 0].astype(F32) + f2[a, 1].astype(F32)
-        ref[:, 0:512] = fin[0:8].astype(BF)
-        ref[:, 512:896] = fin[8:16, 0:384].astype(BF)
+        fin_ref[a, :, 0:512] = fin[0:8].astype(BF)
+        fin_ref[a, :, 512:896] = fin[8:16, 0:384].astype(BF)
 
     hops0 = combine(0, gather(0))
     got = gather(1)
     relay(0, hops0)
     hops1 = combine(1, got)
     relay(1, hops1)
-    finish(0, hops0, mixed_ref)
-    finish(1, hops1, gtok_ref)
+    finish(0, hops0)
+    finish(1, hops1)
 
     for q in pend:
         q.wait_send()
+
+
+def unstack(fin_ref, gr_ref, mixed_ref, gtok_ref, gg_ref, gu_ref, gd_ref, sems):
+    pairs = [(fin_ref.at[0], mixed_ref), (fin_ref.at[1], gtok_ref)]
+    for at, ref in ((0, gg_ref), (304, gu_ref), (640, gd_ref)):
+        pairs.append((gr_ref.at[pl.ds(at, 304)], ref.at[0]))
+    copies = [pltpu.make_async_copy(p, q, sems.at[i]) for i, (p, q) in enumerate(pairs)]
+    for q in copies:
+        q.start()
+    for q in copies:
+        q.wait()
 
 
 def shards(tokens, out_grad, expert_ids, gate_probs, w_gate, w_up, w_down):
     vm = pl.BlockSpec(memory_space=pltpu.VMEM)
     hbm = pl.BlockSpec(memory_space=pltpu.HBM)
     dma = pltpu.SemaphoreType.DMA
-    mixed, gtok, gg, gu, gd = pl.pallas_call(
+    fin, grads = pl.pallas_call(
         kernel,
         out_shape=(
-            jax.ShapeDtypeStruct((8, 896), BF),
-            jax.ShapeDtypeStruct((8, 896), BF),
-            jax.ShapeDtypeStruct((1, 304, 896), BF),
-            jax.ShapeDtypeStruct((1, 304, 896), BF),
-            jax.ShapeDtypeStruct((1, 304, 896), BF),
+            jax.ShapeDtypeStruct((2, 8, 896), BF),
+            jax.ShapeDtypeStruct((1024, 896), BF),
         ),
         in_specs=[vm] * 4 + [hbm] * 3,
-        out_specs=(vm,) * 5,
+        out_specs=(vm,) * 2,
         scratch_shapes=[
             pltpu.VMEM((1024, 896), BF),
             pltpu.VMEM((4, 2, 16, 1024), BF),
@@ -384,7 +390,6 @@
             pltpu.VMEM((2, 2, 16, 256), BF),
             pltpu.VMEM((2, 3, 16, 512), BF),
             pltpu.VMEM((2, 2, 16, 512), BF),
-            pltpu.VMEM((1024, 896), BF),
         ]
         + [dma((6,))] * 2
         + [dma((4,))] * 2
@@ -406,6 +411,20 @@
         tokens, out_grad, expert_ids.T, gate_probs.T,
         w_gate.transpose(0, 2, 1), w_up.transpose(0, 2, 1), w_down,
     )
+    mixed, gtok, gg, gu, gd = pl.pallas_call(
+        unstack,
+        out_shape=(
+            jax.ShapeDtypeStruct((8, 896), BF),
+            jax.ShapeDtypeStruct((8, 896), BF),
+            jax.ShapeDtypeStruct((1, 304, 896), BF),
+            jax.ShapeDtypeStruct((1, 304, 896), BF),
+            jax.ShapeDtypeStruct((1, 304, 896), BF),
+        ),
+        in_specs=[vm] * 2,
+        out_specs=(hbm,) * 5,
+        scratch_shapes=[dma((5,))],
+        compiler_params=pltpu.CompilerParams(vmem_limit_bytes=60 << 20),
+    )(fin, grads)
     return mixed, gtok, gg.transpose(0, 2, 1), gu.transpose(0, 2, 1), gd
 
 

time: 145 us -> 140 us (0.966)
  local copies, waits for them, and re-layouts: 5.92 us -> 0 us
    unnamed x11 -> x0, local copies, waits for them, and re-layouts: 5.92 us -> none
    pallas_call x1 -> x2, Pallas kernels: 138 us -> 139 us  [the longest x1 136 us: shards(): pl.pallas_call(kernel, out_shape=(jax.ShapeDtypeStruct((2, 8, 896), BF),...]
where the time goes in v4:
time: 140 us
  Pallas kernels  139 us (99%)
    pallas_call x1, Pallas kernels, shards(): pl.pallas_call(kernel, out_shape=(jax.ShapeDtypeStruct((2, 8, 896), BF),...  136 us

profile of v4, /device:TPU:1, one launch (start us, length us, event | category | flops | bytes accessed | tf_op | source)
XLA Modules:
  0.0 139.6 jit_solution(14747479111229460603)
XLA Ops:
  0.6 136.3 %shard_map.110 = (bf16[2,8,896]{2,1,0:T(8,128)(2,1)}, bf16[1024,896]{1,0:T(8,128)(2,1)}) custom-call(bf16[8,896]{1,0:T(8,128)(2,1)} %tok_ref.1, bf16[8,896]{1,0:T(8,128)(2,1)} %og_ref.1, s32[2,8]{1,0:T(2,128)} %bitcast.10, f32[2,8]{1,0:T(2,128)} %bitcast.11, bf16[1,304,896]{2,1,0:T(8,128)(2,1)} %bitcast.6, bf16[1,304,896]{2,1,0:T(8,128)(2,1)} %bitcast.7, ...), custom_call_target="tpu_custom_call" | custom-call | flops 2600000000 | bytes 4000000 | tf_op jit(solution)/shard_map/pallas_call | solution.py:367
  136.9 2.7 %shard_map.111 = (bf16[8,896]{1,0:T(8,128)(2,1)}, bf16[8,896]{1,0:T(8,128)(2,1)}, bf16[1,304,896]{2,1,0:T(8,128)(2,1)}, bf16[1,304,896]{2,1,0:T(8,128)(2,1)}, bf16[1,304,896]{2,1,0:T(8,128)(2,1)}) custom-call(bf16[2,8,896]{2,1,0:T(8,128)(2,1)} %get-tuple-element.12.fin_ref, bf16[1024,896]{1,0:T(8,128)(2,1)} %get-tuple-element.13.gr_ref), custom_call_target="tpu_custom_call" | custom-call | tf_op jit(solution)/shard_map/pallas_call | solution.py:414

commit v5 on v4

--- a/solution.py
+++ b/solution.py
@@ -46,10 +46,10 @@
 
 def kernel(
     tok_ref, og_ref, ids_ref, probs_ref, wg_ref, wu_ref, wd_ref,
-    fin_ref, gr,
-    w, zed, sx, xd, ps, rp, hb, os_, ro, sb, rb, ts, rs, fs, f1, fg, f2,
+    fin_ref, grads_ref,
+    w, zed, sx, xd, ps, rp, hb, os_, ro, sb, rb, ts, rs, fs, f1, fg, f2, gr,
     a_s, a_r, s_s, s_r, b_s, b_r, y_s, y_r, v_s, v_r, p_s, p_r, h_s, h_r,
-    o_s, o_r, c_s, c_r, t_s, t_r, f_s, f_r, w_m,
+    o_s, o_r, c_s, c_r, t_s, t_r, f_s, f_r, w_m, g_m,
 ):
     dp = lax.axis_index("dp")
     ex = lax.axis_index("expert")
@@ -268,6 +268,9 @@
     hs = hb[...].reshape(512, 1024)
     for at, n, r in ((0, 256, xs), (256, 256, xs), (512, 128, xs), (640, 384, ds)):
         gr[at : at + n] = tn(hs[:, at : at + n], r).astype(BF)
+    save = pltpu.make_async_copy(gr, grads_ref, g_m)
+    save.start()
+
     def gather(a):
         got = []
         for i in range(8):
@@ -347,6 +350,7 @@
 
     for q in pend:
         q.wait_send()
+    save.wait()
 
 
 def unstack(fin_ref, gr_ref, mixed_ref, gtok_ref, gg_ref, gu_ref, gd_ref, sems):
@@ -371,7 +375,7 @@
             jax.ShapeDtypeStruct((1024, 896), BF),
         ),
         in_specs=[vm] * 4 + [hbm] * 3,
-        out_specs=(vm,) * 2,
+        out_specs=(vm, hbm),
         scratch_shapes=[
             pltpu.VMEM((1024, 896), BF),
             pltpu.VMEM((4, 2, 16, 1024), BF),
@@ -390,6 +394,7 @@
             pltpu.VMEM((2, 2, 16, 256), BF),
             pltpu.VMEM((2, 3, 16, 512), BF),
             pltpu.VMEM((2, 2, 16, 512), BF),
+            pltpu.VMEM((1024, 896), BF),
         ]
         + [dma((6,))] * 2
         + [dma((4,))] * 2
@@ -400,7 +405,7 @@
         + [dma((2, 7))] * 2
         + [dma((2,))] * 2
         + [dma((2, 6))] * 2
-        + [dma((3,))],
+        + [dma((3,)), dma],
         compiler_params=pltpu.CompilerParams(
             collective_id=0, has_side_effects=True, vmem_limit_bytes=60 << 20
         ),

time: 140 us -> 139 us (level)
  no operation moved by 1% of the time
where the time goes in v5:
time: 139 us
  Pallas kernels  138 us (99%)
    pallas_call x1, Pallas kernels, shards(): pl.pallas_call(kernel, out_shape=(jax.ShapeDtypeStruct((2, 8, 896), BF),...  136 us

profile of v5, /device:TPU:1, one launch (start us, length us, event | category | flops | bytes accessed | tf_op | source)
XLA Modules:
  0.0 139.0 jit_solution(6879263493765637510)
XLA Ops:
  0.6 135.7 %shard_map.110 = (bf16[2,8,896]{2,1,0:T(8,128)(2,1)}, bf16[1024,896]{1,0:T(8,128)(2,1)}) custom-call(bf16[8,896]{1,0:T(8,128)(2,1)} %tok_ref.1, bf16[8,896]{1,0:T(8,128)(2,1)} %og_ref.1, s32[2,8]{1,0:T(2,128)} %bitcast.10, f32[2,8]{1,0:T(2,128)} %bitcast.11, bf16[1,304,896]{2,1,0:T(8,128)(2,1)} %bitcast.6, bf16[1,304,896]{2,1,0:T(8,128)(2,1)} %bitcast.7, ...), custom_call_target="tpu_custom_call" | custom-call | flops 2600000000 | bytes 4000000 | tf_op jit(solution)/shard_map/pallas_call | solution.py:371
  136.3 2.7 %shard_map.111 = (bf16[8,896]{1,0:T(8,128)(2,1)}, bf16[8,896]{1,0:T(8,128)(2,1)}, bf16[1,304,896]{2,1,0:T(8,128)(2,1)}, bf16[1,304,896]{2,1,0:T(8,128)(2,1)}, bf16[1,304,896]{2,1,0:T(8,128)(2,1)}) custom-call(bf16[2,8,896]{2,1,0:T(8,128)(2,1)} %get-tuple-element.12.fin_ref, bf16[1024,896]{1,0:T(8,128)(2,1)} %get-tuple-element.13.gr_ref), custom_call_target="tpu_custom_call" | custom-call | tf_op jit(solution)/shard_map/pallas_call | solution.py:419
